TPU v7x, 32 devices: a whole 2x2x4 slice. The times are simulated.
32 devices in a mesh: ctx: 8 (over z, core), head: 4 (over y, x).
Axes of the slice: x: 2, y: 2, z: 4, core: 2. Of those that a mesh axis runs over, the one named last changes fastest.
Arguments:
- queries: bfloat16 [2048, 32, 128], P('ctx', 'head'), may hold values from -8 to 8
- key_proj: bfloat16 [2048, 4, 128], P(('ctx', 'head')), may hold values from -8 to 8
- value_proj: bfloat16 [2048, 4, 128], P(('ctx', 'head')), may hold values from -6 to 6
- out_grad: bfloat16 [2048, 32, 128], P('ctx', 'head'), may hold values from -6 to 6
- tile_order: int32 [16], replicated, may hold values from 0 to 15, each once
- doc_tiles: int32 [4], replicated, may hold values from 1 to 8, 16 in all
Outputs:
- attended: bfloat16 [2048, 32, 128], P('ctx', 'head')
- query_grad: bfloat16 [2048, 32, 128], P('ctx', 'head')
- key_grad: bfloat16 [2048, 4, 128], P(('ctx', 'head'))
- value_grad: bfloat16 [2048, 4, 128], P(('ctx', 'head'))
Inputs may be any that keep to these rules, and one draw needn't show every extreme that they name: `tile_order`: a permutation of the 16 tiles. `doc_tiles`: positive lengths in tiles summing to 16.
All inputs are finite; a program needn't handle non-finite values.
Results may differ from a plain program's by a relative error of at most 0.02.
Values may be sent and summed in bfloat16 or wider, within the bound.
A program may use at most 64 MiB of HBM per device.

v0:
```python
import math
import jax
import jax.numpy as jnp
from jax import lax
from jax.sharding import PartitionSpec as P

TILE = 128
NEG = -1e30


def from_behind(value, axis, steps):
    count = lax.axis_size(axis)
    pairs = [(source, (source + steps) % count) for source in range(count)]
    return lax.ppermute(value, axis, pairs)


def row_info(tile_order, doc_ends, shard, row_count, tile_len):
    per_shard = row_count // tile_len
    shard_tiles = lax.dynamic_slice_in_dim(tile_order, shard * per_shard, per_shard)
    tile_doc = jnp.sum((shard_tiles[:, None] >= doc_ends[None, :]).astype(jnp.int32), axis=1)
    offsets = jnp.arange(tile_len, dtype=jnp.int32)
    positions = (shard_tiles[:, None] * tile_len + offsets[None, :]).reshape(-1)
    documents = jnp.broadcast_to(tile_doc[:, None], (per_shard, tile_len)).reshape(-1)
    return (positions, documents, shard_tiles, tile_doc)


def block_scores(query_block, key_block, score_scale):
    return (
        jnp.einsum("tngd,knd->tngk", query_block, key_block, preferred_element_type=jnp.float32)
        * score_scale
    )


def forward_block(carried, query_block, key_block, value_block, allowed, score_scale):
    running_max, running_sum, accumulated = carried
    scores = block_scores(query_block, key_block, score_scale)
    visible = allowed[:, None, None, :]
    block_max = jnp.max(jnp.where(visible, scores, NEG), axis=-1)
    new_max = jnp.maximum(running_max, block_max)
    weights = jnp.where(visible, jnp.exp(scores - new_max[..., None]), 0.0)
    factor = jnp.exp(running_max - new_max)
    running_sum = running_sum * factor + jnp.sum(weights, axis=-1)
    product = jnp.einsum(
        "tngk,knd->tngd",
        weights.astype(jnp.bfloat16),
        value_block,
        preferred_element_type=jnp.float32,
    )
    accumulated = accumulated * factor[..., None] + product
    return (new_max, running_sum, accumulated)


def backward_block(
    query_block, grad_block, log_sum, delta, key_block, value_block, allowed, score_scale
):
    scores = block_scores(query_block, key_block, score_scale)
    visible = allowed[:, None, None, :]
    probs = jnp.where(visible, jnp.exp(scores - log_sum[..., None]), 0.0)
    value_add = jnp.einsum(
        "tngk,tngd->knd", probs.astype(jnp.bfloat16), grad_block, preferred_element_type=jnp.float32
    )
    dprobs = jnp.einsum(
        "tngd,knd->tngk", grad_block, value_block, preferred_element_type=jnp.float32
    )
    dscores = (probs * (dprobs - delta[..., None])).astype(jnp.bfloat16)
    query_add = jnp.einsum("tngk,knd->tngd", dscores, key_block, preferred_element_type=jnp.float32)
    key_add = jnp.einsum("tngk,tngd->knd", dscores, query_block, preferred_element_type=jnp.float32)
    return (query_add, key_add, value_add)


def body(queries, key_proj, value_proj, out_grad, tile_order, doc_tiles):
    key_rows, value_rows = (
        lax.all_to_all(key_proj, "head", split_axis=1, concat_axis=0, tiled=True),
        lax.all_to_all(value_proj, "head", split_axis=1, concat_axis=0, tiled=True),
    )
    row_count = queries.shape[0]
    kv_local = key_rows.shape[1]
    group_size = queries.shape[1] // kv_local
    depth = queries.shape[2]
    query_rows = queries.reshape(row_count, kv_local, group_size, depth)
    grad_rows = out_grad.reshape(row_count, kv_local, group_size, depth)
    score_scale = 1.0 / math.sqrt(depth)
    cycle_size = lax.axis_size("ctx")
    my_shard = lax.axis_index("ctx")
    doc_ends = jnp.cumsum(doc_tiles)
    query_pos, query_doc, query_tiles, query_tdoc = row_info(
        tile_order, doc_ends, my_shard, row_count, TILE
    )

    def block_mask(shard):
        key_pos, key_doc, key_tiles, key_tdoc = row_info(
            tile_order, doc_ends, shard, row_count, TILE
        )
        allowed = (query_doc[:, None] == key_doc[None, :]) & (
            key_pos[None, :] <= query_pos[:, None]
        )
        reached = jnp.any(
            (query_tdoc[:, None] == key_tdoc[None, :])
            & (key_tiles[None, :] <= query_tiles[:, None])
        )
        return (allowed, reached)

    def forward_step(carried, key_block, value_block, shard):
        allowed, reached = block_mask(shard)
        return forward_block(carried, query_rows, key_block, value_block, allowed, score_scale)

    stats_shape = (row_count, kv_local, group_size)
    initial = (
        jnp.full(stats_shape, NEG, jnp.float32),
        jnp.zeros(stats_shape, jnp.float32),
        jnp.zeros(stats_shape + (depth,), jnp.float32),
    )
    first = forward_step(initial, key_rows, value_rows, my_shard)

    def forward_turn(turn_index, carried):
        key_block, value_block = from_behind((carried[0], carried[1]), "ctx", 1)
        shard = (my_shard - turn_index) % cycle_size
        return (key_block, value_block, forward_step(carried[2], key_block, value_block, shard))

    finished = lax.fori_loop(1, cycle_size, forward_turn, (key_rows, value_rows, first))
    running_max, running_sum, accumulated = finished[2]
    attended = (accumulated / running_sum[..., None]).astype(jnp.bfloat16)
    log_sum = running_max + jnp.log(running_sum)
    delta = jnp.sum(grad_rows.astype(jnp.float32) * attended.astype(jnp.float32), axis=-1)

    def backward_step(key_block, value_block, shard):
        allowed, reached = block_mask(shard)
        return backward_block(
            query_rows, grad_rows, log_sum, delta, key_block, value_block, allowed, score_scale
        )

    query_acc = jnp.zeros(stats_shape + (depth,), jnp.float32)

    def backward_turn(turn_index, carried):
        key_block, value_block, key_acc, value_acc, query_sum = carried
        shard = (my_shard - turn_index) % cycle_size
        query_add, key_add, value_add = backward_step(key_block, value_block, shard)
        key_block, value_block = from_behind((key_block, value_block), "ctx", 1)
        key_acc, value_acc = (
            from_behind((key_acc + key_add).astype(jnp.bfloat16), "ctx", 1).astype(jnp.float32),
            from_behind((value_acc + value_add).astype(jnp.bfloat16), "ctx", 1).astype(jnp.float32),
        )
        return (key_block, value_block, key_acc, value_acc, query_sum + query_add)

    grad_zero = jnp.zeros((row_count, kv_local, depth), jnp.float32)
    finished = lax.fori_loop(
        0, cycle_size, backward_turn, (key_rows, value_rows, grad_zero, grad_zero, query_acc)
    )
    key_acc, value_acc, query_acc = (finished[2], finished[3], finished[4])
    query_grad = (
        (query_acc * score_scale)
        .astype(jnp.bfloat16)
        .reshape(row_count, kv_local * group_size, depth)
    )
    key_grad = (key_acc * score_scale).astype(jnp.bfloat16)
    value_grad = value_acc.astype(jnp.bfloat16)
    attended = attended.reshape(row_count, kv_local * group_size, depth)
    key_back, value_back = (
        lax.all_to_all(key_grad, "head", split_axis=0, concat_axis=1, tiled=True),
        lax.all_to_all(value_grad, "head", split_axis=0, concat_axis=1, tiled=True),
    )
    return (attended, query_grad, key_back, value_back)


def solution(mesh):
    in_specs = (
        P("ctx", "head", None),
        P(("ctx", "head"), None, None),
        P(("ctx", "head"), None, None),
        P("ctx", "head", None),
        P(),
        P(),
    )
    out_specs = (
        P("ctx", "head", None),
        P("ctx", "head", None),
        P(("ctx", "head"), None, None),
        P(("ctx", "head"), None, None),
    )
    return jax.shard_map(body, mesh=mesh, in_specs=in_specs, out_specs=out_specs, check_vma=False)
```

profile of v0, /device:TPU:0, one launch (start us, length us, event | category | flops | bytes accessed | tf_op | source)
XLA Modules:
  0.0 183.4 jit_solution(8842191101418843890)
XLA Ops:
  0.6 1.5 copy.74
  2.2 5.2 %all-to-all-start = ((bf16[64,4,128]{2,0,1:T(8,128)(2,1)}), bf16[64,4,128]{2,0,1:T(8,128)(2,1)S(1)}, u32[]{:S(2)}, u32[]{:S(2)}) async-start(bf16[64,4,128]{2,0,1:T(8,128)(2,1)} %copy.74), calls=%async_computation | async-start | bytes 131072 | tf_op jit(solution)/shard_map/all_to_all | solution.py:73
  9.6 1.5 copy.75
  12.2 3.3 %all-to-all-start.1 = ((bf16[64,4,128]{2,0,1:T(8,128)(2,1)}), bf16[64,4,128]{2,0,1:T(8,128)(2,1)S(1)}, u32[]{:S(2)}, u32[]{:S(2)}) async-start(bf16[64,4,128]{2,0,1:T(8,128)(2,1)} %copy.75), calls=%async_computation.1 | async-start | bytes 131072 | tf_op jit(solution)/shard_map/all_to_all | solution.py:74
  18.5 1.8 all-to-all-done.1
  22.9 62.3 %while.48 = (s32[]{:T(128)}, bf16[256,1,128]{2,0,1:T(8,128)(2,1)}, bf16[256,1,128]{2,0,1:T(8,128)(2,1)}, f32[256,1,8]{0,2,1:T(8,128)S(1)}, f32[256,1,8]{0,2,1:T(...) while((s32[]{:T(128)}, bf16[256,1,128]{2,0,1:T(8,128)(2,1)}, ...), condition=%wide.region_8.9_spmd.clone, body=%wide.region_4.0_spmd.clone.sunk | while | flops 274930240 | bytes 10232312 | solution.py:120
  22.9 1.7 collective-permute-start.1
  24.6 1.3 add_bitcast_fusion.9
  31.8 1.5 collective-permute-start.1
  33.3 1.3 add_bitcast_fusion.9
  40.7 1.3 collective-permute-start.1
  42.0 1.3 add_bitcast_fusion.9
  49.7 1.3 add_bitcast_fusion.9
  53.5 1.8 collective-permute-done
  58.6 1.3 add_bitcast_fusion.9
  62.4 1.8 collective-permute-done
  67.5 1.3 add_bitcast_fusion.9
  71.3 1.8 collective-permute-done
  76.4 1.3 add_bitcast_fusion.9
  80.2 1.8 collective-permute-done
  86.6 3.3 %multiply_reduce_fusion = (f32[256,8]{1,0:T(8,128)}, bf16[256,1,8,128]{3,2,0,1:T(8,128)(2,1)}) fusion(bf16[256,8,128]{2,1,0:T(8,128)(2,1)} %param.13, f32[256,8]{1,0:T(8,128)} %copy.79, f32[256,1,8,128]{3,0,2,1:T(8,128)S(1)} %get-tuple-element.648), kind=kLoop, calls=%fused_computation.83 | loop fusion | flops 1570816 | bytes 2113536 | tf_op jit(solution)/shard_map/reduce_sum | solution.py:124
  90.9 73.6 %while.49 = (s32[]{:T(128)}, bf16[256,1,128]{2,0,1:T(8,128)(2,1)S(1)}, bf16[256,1,128]{2,0,1:T(8,128)(2,1)S(1)}, f32[256,1,128]{2,0,1:T(8,128)S(1)}, f32[256,1,1...) while((s32[]{:T(128)}, ...), condition=%wide.region_12.13_spmd.clone, body=%wide.region_10.12_spmd.clone.sunk | while | flops 675742272 | bytes 16081516 | solution.py:146
  91.7 1.3 bitcast_select_fusion.4
  94.4 1.6 collective-permute-start.5
  96.8 2.6 %collective-permute-done.4 = bf16[256,1,128]{2,0,1:T(8,128)(2,1)S(1)} collective-permute-done((bf16[256,1,128]{2,0,1:T(8,128)(2,1)S(1)}, bf16[256,1,128]{2,0,1:T(8,128)(2,1)S(1)}, u32[]{:S(2)}, u32[]{:S(2)}) %collective-permute-start.4) | collective-permute-done | bytes 65568 | tf_op jit(solution)/shard_map/while/body/eval_jaxpr/ppermute | solution.py:14
  100.9 1.3 bitcast_select_fusion.4
  103.6 1.6 collective-permute-start.5
  106.0 2.6 %collective-permute-done.4 = bf16[256,1,128]{2,0,1:T(8,128)(2,1)S(1)} collective-permute-done((bf16[256,1,128]{2,0,1:T(8,128)(2,1)S(1)}, bf16[256,1,128]{2,0,1:T(8,128)(2,1)S(1)}, u32[]{:S(2)}, u32[]{:S(2)}) %collective-permute-start.4) | collective-permute-done | bytes 65568 | tf_op jit(solution)/shard_map/while/body/eval_jaxpr/ppermute | solution.py:14
  110.1 1.3 bitcast_select_fusion.4
  112.8 1.5 collective-permute-start.5
  115.2 2.6 %collective-permute-done.4 = bf16[256,1,128]{2,0,1:T(8,128)(2,1)S(1)} collective-permute-done((bf16[256,1,128]{2,0,1:T(8,128)(2,1)S(1)}, bf16[256,1,128]{2,0,1:T(8,128)(2,1)S(1)}, u32[]{:S(2)}, u32[]{:S(2)}) %collective-permute-start.4) | collective-permute-done | bytes 65568 | tf_op jit(solution)/shard_map/while/body/eval_jaxpr/ppermute | solution.py:14
  119.3 1.3 bitcast_select_fusion.4
  122.0 1.5 collective-permute-start.5
  124.4 2.6 %collective-permute-done.4 = bf16[256,1,128]{2,0,1:T(8,128)(2,1)S(1)} collective-permute-done((bf16[256,1,128]{2,0,1:T(8,128)(2,1)S(1)}, bf16[256,1,128]{2,0,1:T(8,128)(2,1)S(1)}, u32[]{:S(2)}, u32[]{:S(2)}) %collective-permute-start.4) | collective-permute-done | bytes 65568 | tf_op jit(solution)/shard_map/while/body/eval_jaxpr/ppermute | solution.py:14
  131.2 1.5 collective-permute-start.5
  133.6 2.6 %collective-permute-done.4 = bf16[256,1,128]{2,0,1:T(8,128)(2,1)S(1)} collective-permute-done((bf16[256,1,128]{2,0,1:T(8,128)(2,1)S(1)}, bf16[256,1,128]{2,0,1:T(8,128)(2,1)S(1)}, u32[]{:S(2)}, u32[]{:S(2)}) %collective-permute-start.4) | collective-permute-done | bytes 65568 | tf_op jit(solution)/shard_map/while/body/eval_jaxpr/ppermute | solution.py:14
  137.7 1.3 bitcast_select_fusion.4
  140.4 1.5 collective-permute-start.5
  142.8 2.6 %collective-permute-done.4 = bf16[256,1,128]{2,0,1:T(8,128)(2,1)S(1)} collective-permute-done((bf16[256,1,128]{2,0,1:T(8,128)(2,1)S(1)}, bf16[256,1,128]{2,0,1:T(8,128)(2,1)S(1)}, u32[]{:S(2)}, u32[]{:S(2)}) %collective-permute-start.4) | collective-permute-done | bytes 65568 | tf_op jit(solution)/shard_map/while/body/eval_jaxpr/ppermute | solution.py:14
  149.6 1.5 collective-permute-start.5
  152.0 2.6 %collective-permute-done.4 = bf16[256,1,128]{2,0,1:T(8,128)(2,1)S(1)} collective-permute-done((bf16[256,1,128]{2,0,1:T(8,128)(2,1)S(1)}, bf16[256,1,128]{2,0,1:T(8,128)(2,1)S(1)}, u32[]{:S(2)}, u32[]{:S(2)}) %collective-permute-start.4) | collective-permute-done | bytes 65568 | tf_op jit(solution)/shard_map/while/body/eval_jaxpr/ppermute | solution.py:14
  158.8 1.5 collective-permute-start.5
  161.2 2.6 %collective-permute-done.4 = bf16[256,1,128]{2,0,1:T(8,128)(2,1)S(1)} collective-permute-done((bf16[256,1,128]{2,0,1:T(8,128)(2,1)S(1)}, bf16[256,1,128]{2,0,1:T(8,128)(2,1)S(1)}, u32[]{:S(2)}, u32[]{:S(2)}) %collective-permute-start.4) | collective-permute-done | bytes 65568 | tf_op jit(solution)/shard_map/while/body/eval_jaxpr/ppermute | solution.py:14
  166.4 3.3 %all-to-all-start.2 = ((bf16[4,2,4096]{2,1,0:T(2,128)(2,1)}), bf16[4,2,4096]{2,1,0:T(2,128)(2,1)S(1)}, u32[]{:S(2)}, u32[]{:S(2)}) async-start(bf16[4,2,4096]{2,1,0:T(2,128)(2,1)} %reshape.646), calls=%async_computation.2 | async-start | bytes 131072 | tf_op jit(solution)/shard_map/all_to_all | solution.py:159
  171.1 3.5 %all-to-all-done.2 = bf16[4,2,4096]{2,1,0:T(2,128)(2,1)S(1)} async-done(((bf16[4,2,4096]{2,1,0:T(2,128)(2,1)}), bf16[4,2,4096]{2,1,0:T(2,128)(2,1)S(1)}, u32[]{:S(2)}, u32[]{:S(2)}) %all-to-all-start.2) | async-done | bytes 65568 | tf_op jit(solution)/shard_map/all_to_all | solution.py:159
  174.5 3.3 %all-to-all-start.3 = ((bf16[4,2,4096]{2,1,0:T(2,128)(2,1)}), bf16[4,2,4096]{2,1,0:T(2,128)(2,1)S(1)}, u32[]{:S(2)}, u32[]{:S(2)}) async-start(bf16[4,2,4096]{2,1,0:T(2,128)(2,1)} %reshape.648), calls=%async_computation.3 | async-start | bytes 131072 | tf_op jit(solution)/shard_map/all_to_all | solution.py:160
  177.8 1.5 fusion.61
  180.1 2.6 %all-to-all-done.3 = bf16[4,2,4096]{2,1,0:T(2,128)(2,1)S(1)} async-done(((bf16[4,2,4096]{2,1,0:T(2,128)(2,1)}), bf16[4,2,4096]{2,1,0:T(2,128)(2,1)S(1)}, u32[]{:S(2)}, u32[]{:S(2)}) %all-to-all-start.3) | async-done | bytes 65568 | tf_op jit(solution)/shard_map/all_to_all | solution.py:160
  (318 shorter events, 89.7 us)
Async XLA Ops:
  2.2 10.0 %all-to-all-start = ((bf16[64,4,128]{2,0,1:T(8,128)(2,1)}), bf16[64,4,128]{2,0,1:T(8,128)(2,1)S(1)}, u32[]{:S(2)}, u32[]{:S(2)}) async-start(bf16[64,4,128]{2,0,1:T(8,128)(2,1)} %copy.74), calls=%async_computation | async-start | bytes 131072 | tf_op jit(solution)/shard_map/all_to_all | solution.py:73
  12.2 8.1 %all-to-all-start.1 = ((bf16[64,4,128]{2,0,1:T(8,128)(2,1)}), bf16[64,4,128]{2,0,1:T(8,128)(2,1)S(1)}, u32[]{:S(2)}, u32[]{:S(2)}) async-start(bf16[64,4,128]{2,0,1:T(8,128)(2,1)} %copy.75), calls=%async_computation.1 | async-start | bytes 131072 | tf_op jit(solution)/shard_map/all_to_all | solution.py:74
  22.9 5.8 %collective-permute-start = (bf16[256,1,128]{2,0,1:T(8,128)(2,1)}, bf16[256,1,128]{2,0,1:T(8,128)(2,1)S(1)}, u32[]{:S(2)}, u32[]{:S(2)}) collective-permute-start(bf16[256,1,128]{2,0,1:T(8,128)(2,1)} %get-tuple-element.1124), channel_id=1, source_target_pairs={{0,4},{4,8},{8,12},{12,16},{16,20},{20,24},{24,28},{28,0},{1,5},{5... | collective-permute-start | bytes 196616 | tf_op jit(solution)/shard_map/while/body/eval_jaxpr/ppermute | solution.py:14
  22.9 7.3 %collective-permute-start.1 = (bf16[256,1,128]{2,0,1:T(8,128)(2,1)}, bf16[256,1,128]{2,0,1:T(8,128)(2,1)S(1)}, u32[]{:S(2)}, u32[]{:S(2)}) collective-permute-start(bf16[256,1,128]{2,0,1:T(8,128)(2,1)} %get-tuple-element.1125), channel_id=1, source_target_pairs={{0,4},{4,8},{8,12},{12,16},{16,20},{20,24},{24,28},{28,0},{1,5},{5... | collective-permute-start | bytes 196616 | tf_op jit(solution)/shard_map/while/body/eval_jaxpr/ppermute | solution.py:14
  31.8 5.8 %collective-permute-start = (bf16[256,1,128]{2,0,1:T(8,128)(2,1)}, bf16[256,1,128]{2,0,1:T(8,128)(2,1)S(1)}, u32[]{:S(2)}, u32[]{:S(2)}) collective-permute-start(bf16[256,1,128]{2,0,1:T(8,128)(2,1)} %get-tuple-element.1124), channel_id=1, source_target_pairs={{0,4},{4,8},{8,12},{12,16},{16,20},{20,24},{24,28},{28,0},{1,5},{5... | collective-permute-start | bytes 196616 | tf_op jit(solution)/shard_map/while/body/eval_jaxpr/ppermute | solution.py:14
  31.8 7.3 %collective-permute-start.1 = (bf16[256,1,128]{2,0,1:T(8,128)(2,1)}, bf16[256,1,128]{2,0,1:T(8,128)(2,1)S(1)}, u32[]{:S(2)}, u32[]{:S(2)}) collective-permute-start(bf16[256,1,128]{2,0,1:T(8,128)(2,1)} %get-tuple-element.1125), channel_id=1, source_target_pairs={{0,4},{4,8},{8,12},{12,16},{16,20},{20,24},{24,28},{28,0},{1,5},{5... | collective-permute-start | bytes 196616 | tf_op jit(solution)/shard_map/while/body/eval_jaxpr/ppermute | solution.py:14
  40.7 5.8 %collective-permute-start = (bf16[256,1,128]{2,0,1:T(8,128)(2,1)}, bf16[256,1,128]{2,0,1:T(8,128)(2,1)S(1)}, u32[]{:S(2)}, u32[]{:S(2)}) collective-permute-start(bf16[256,1,128]{2,0,1:T(8,128)(2,1)} %get-tuple-element.1124), channel_id=1, source_target_pairs={{0,4},{4,8},{8,12},{12,16},{16,20},{20,24},{24,28},{28,0},{1,5},{5... | collective-permute-start | bytes 196616 | tf_op jit(solution)/shard_map/while/body/eval_jaxpr/ppermute | solution.py:14
  40.7 7.3 %collective-permute-start.1 = (bf16[256,1,128]{2,0,1:T(8,128)(2,1)}, bf16[256,1,128]{2,0,1:T(8,128)(2,1)S(1)}, u32[]{:S(2)}, u32[]{:S(2)}) collective-permute-start(bf16[256,1,128]{2,0,1:T(8,128)(2,1)} %get-tuple-element.1125), channel_id=1, source_target_pairs={{0,4},{4,8},{8,12},{12,16},{16,20},{20,24},{24,28},{28,0},{1,5},{5... | collective-permute-start | bytes 196616 | tf_op jit(solution)/shard_map/while/body/eval_jaxpr/ppermute | solution.py:14
  49.6 5.8 %collective-permute-start = (bf16[256,1,128]{2,0,1:T(8,128)(2,1)}, bf16[256,1,128]{2,0,1:T(8,128)(2,1)S(1)}, u32[]{:S(2)}, u32[]{:S(2)}) collective-permute-start(bf16[256,1,128]{2,0,1:T(8,128)(2,1)} %get-tuple-element.1124), channel_id=1, source_target_pairs={{0,4},{4,8},{8,12},{12,16},{16,20},{20,24},{24,28},{28,0},{1,5},{5... | collective-permute-start | bytes 196616 | tf_op jit(solution)/shard_map/while/body/eval_jaxpr/ppermute | solution.py:14
  49.6 7.3 %collective-permute-start.1 = (bf16[256,1,128]{2,0,1:T(8,128)(2,1)}, bf16[256,1,128]{2,0,1:T(8,128)(2,1)S(1)}, u32[]{:S(2)}, u32[]{:S(2)}) collective-permute-start(bf16[256,1,128]{2,0,1:T(8,128)(2,1)} %get-tuple-element.1125), channel_id=1, source_target_pairs={{0,4},{4,8},{8,12},{12,16},{16,20},{20,24},{24,28},{28,0},{1,5},{5... | collective-permute-start | bytes 196616 | tf_op jit(solution)/shard_map/while/body/eval_jaxpr/ppermute | solution.py:14
  58.5 5.8 %collective-permute-start = (bf16[256,1,128]{2,0,1:T(8,128)(2,1)}, bf16[256,1,128]{2,0,1:T(8,128)(2,1)S(1)}, u32[]{:S(2)}, u32[]{:S(2)}) collective-permute-start(bf16[256,1,128]{2,0,1:T(8,128)(2,1)} %get-tuple-element.1124), channel_id=1, source_target_pairs={{0,4},{4,8},{8,12},{12,16},{16,20},{20,24},{24,28},{28,0},{1,5},{5... | collective-permute-start | bytes 196616 | tf_op jit(solution)/shard_map/while/body/eval_jaxpr/ppermute | solution.py:14
  58.5 7.3 %collective-permute-start.1 = (bf16[256,1,128]{2,0,1:T(8,128)(2,1)}, bf16[256,1,128]{2,0,1:T(8,128)(2,1)S(1)}, u32[]{:S(2)}, u32[]{:S(2)}) collective-permute-start(bf16[256,1,128]{2,0,1:T(8,128)(2,1)} %get-tuple-element.1125), channel_id=1, source_target_pairs={{0,4},{4,8},{8,12},{12,16},{16,20},{20,24},{24,28},{28,0},{1,5},{5... | collective-permute-start | bytes 196616 | tf_op jit(solution)/shard_map/while/body/eval_jaxpr/ppermute | solution.py:14
  67.4 5.8 %collective-permute-start = (bf16[256,1,128]{2,0,1:T(8,128)(2,1)}, bf16[256,1,128]{2,0,1:T(8,128)(2,1)S(1)}, u32[]{:S(2)}, u32[]{:S(2)}) collective-permute-start(bf16[256,1,128]{2,0,1:T(8,128)(2,1)} %get-tuple-element.1124), channel_id=1, source_target_pairs={{0,4},{4,8},{8,12},{12,16},{16,20},{20,24},{24,28},{28,0},{1,5},{5... | collective-permute-start | bytes 196616 | tf_op jit(solution)/shard_map/while/body/eval_jaxpr/ppermute | solution.py:14
  67.4 7.3 %collective-permute-start.1 = (bf16[256,1,128]{2,0,1:T(8,128)(2,1)}, bf16[256,1,128]{2,0,1:T(8,128)(2,1)S(1)}, u32[]{:S(2)}, u32[]{:S(2)}) collective-permute-start(bf16[256,1,128]{2,0,1:T(8,128)(2,1)} %get-tuple-element.1125), channel_id=1, source_target_pairs={{0,4},{4,8},{8,12},{12,16},{16,20},{20,24},{24,28},{28,0},{1,5},{5... | collective-permute-start | bytes 196616 | tf_op jit(solution)/shard_map/while/body/eval_jaxpr/ppermute | solution.py:14
  76.3 5.8 %collective-permute-start = (bf16[256,1,128]{2,0,1:T(8,128)(2,1)}, bf16[256,1,128]{2,0,1:T(8,128)(2,1)S(1)}, u32[]{:S(2)}, u32[]{:S(2)}) collective-permute-start(bf16[256,1,128]{2,0,1:T(8,128)(2,1)} %get-tuple-element.1124), channel_id=1, source_target_pairs={{0,4},{4,8},{8,12},{12,16},{16,20},{20,24},{24,28},{28,0},{1,5},{5... | collective-permute-start | bytes 196616 | tf_op jit(solution)/shard_map/while/body/eval_jaxpr/ppermute | solution.py:14
  76.3 7.3 %collective-permute-start.1 = (bf16[256,1,128]{2,0,1:T(8,128)(2,1)}, bf16[256,1,128]{2,0,1:T(8,128)(2,1)S(1)}, u32[]{:S(2)}, u32[]{:S(2)}) collective-permute-start(bf16[256,1,128]{2,0,1:T(8,128)(2,1)} %get-tuple-element.1125), channel_id=1, source_target_pairs={{0,4},{4,8},{8,12},{12,16},{16,20},{20,24},{24,28},{28,0},{1,5},{5... | collective-permute-start | bytes 196616 | tf_op jit(solution)/shard_map/while/body/eval_jaxpr/ppermute | solution.py:14
  91.0 9.2 %collective-permute-start.2 = (bf16[256,1,128]{2,0,1:T(8,128)(2,1)S(1)}, bf16[256,1,128]{2,0,1:T(8,128)(2,1)S(1)}, u32[]{:S(2)}, u32[]{:S(2)}) collective-permute-start(bf16[256,1,128]{2,0,1:T(8,128)(2,1)S(1)} %copy.135), channel_id=1, source_target_pairs={{0,4},{4,8},{8,12},{12,16},{16,20},{20,24},{24,28},{28,0},{1,5},{5... | collective-permute-start | bytes 196616 | tf_op jit(solution)/shard_map/while/body/eval_jaxpr/ppermute | solution.py:14
  91.0 9.1 %collective-permute-start.3 = (bf16[256,1,128]{2,0,1:T(8,128)(2,1)S(1)}, bf16[256,1,128]{2,0,1:T(8,128)(2,1)S(1)}, u32[]{:S(2)}, u32[]{:S(2)}) collective-permute-start(bf16[256,1,128]{2,0,1:T(8,128)(2,1)S(1)} %copy.136), channel_id=1, source_target_pairs={{0,4},{4,8},{8,12},{12,16},{16,20},{20,24},{24,28},{28,0},{1,5},{5... | collective-permute-start | bytes 196616 | tf_op jit(solution)/shard_map/while/body/eval_jaxpr/ppermute | solution.py:14
  93.9 5.5 %collective-permute-start.4 = (bf16[256,1,128]{2,0,1:T(8,128)(2,1)S(1)}, bf16[256,1,128]{2,0,1:T(8,128)(2,1)S(1)}, u32[]{:S(2)}, u32[]{:S(2)}) collective-permute-start(bf16[256,1,128]{2,0,1:T(8,128)(2,1)S(1)} %fusion.114), channel_id=1, source_target_pairs={{0,4},{4,8},{8,12},{12,16},{16,20},{20,24},{24,28},{28,0},{1,5},{5... | collective-permute-start | bytes 196616 | tf_op jit(solution)/shard_map/while/body/eval_jaxpr/ppermute | solution.py:14
  94.4 5.7 %collective-permute-start.5 = (bf16[256,1,128]{2,0,1:T(8,128)(2,1)S(1)}, bf16[256,1,128]{2,0,1:T(8,128)(2,1)S(1)}, u32[]{:S(2)}, u32[]{:S(2)}) collective-permute-start(bf16[256,1,128]{2,0,1:T(8,128)(2,1)S(1)} %fusion.115), channel_id=1, source_target_pairs={{0,4},{4,8},{8,12},{12,16},{16,20},{20,24},{24,28},{28,0},{1,5},{5... | collective-permute-start | bytes 196616 | tf_op jit(solution)/shard_map/while/body/eval_jaxpr/ppermute | solution.py:14
  100.2 9.2 %collective-permute-start.2 = (bf16[256,1,128]{2,0,1:T(8,128)(2,1)S(1)}, bf16[256,1,128]{2,0,1:T(8,128)(2,1)S(1)}, u32[]{:S(2)}, u32[]{:S(2)}) collective-permute-start(bf16[256,1,128]{2,0,1:T(8,128)(2,1)S(1)} %copy.135), channel_id=1, source_target_pairs={{0,4},{4,8},{8,12},{12,16},{16,20},{20,24},{24,28},{28,0},{1,5},{5... | collective-permute-start | bytes 196616 | tf_op jit(solution)/shard_map/while/body/eval_jaxpr/ppermute | solution.py:14
  100.3 9.1 %collective-permute-start.3 = (bf16[256,1,128]{2,0,1:T(8,128)(2,1)S(1)}, bf16[256,1,128]{2,0,1:T(8,128)(2,1)S(1)}, u32[]{:S(2)}, u32[]{:S(2)}) collective-permute-start(bf16[256,1,128]{2,0,1:T(8,128)(2,1)S(1)} %copy.136), channel_id=1, source_target_pairs={{0,4},{4,8},{8,12},{12,16},{16,20},{20,24},{24,28},{28,0},{1,5},{5... | collective-permute-start | bytes 196616 | tf_op jit(solution)/shard_map/while/body/eval_jaxpr/ppermute | solution.py:14
  103.1 5.5 %collective-permute-start.4 = (bf16[256,1,128]{2,0,1:T(8,128)(2,1)S(1)}, bf16[256,1,128]{2,0,1:T(8,128)(2,1)S(1)}, u32[]{:S(2)}, u32[]{:S(2)}) collective-permute-start(bf16[256,1,128]{2,0,1:T(8,128)(2,1)S(1)} %fusion.114), channel_id=1, source_target_pairs={{0,4},{4,8},{8,12},{12,16},{16,20},{20,24},{24,28},{28,0},{1,5},{5... | collective-permute-start | bytes 196616 | tf_op jit(solution)/shard_map/while/body/eval_jaxpr/ppermute | solution.py:14
  103.6 5.7 %collective-permute-start.5 = (bf16[256,1,128]{2,0,1:T(8,128)(2,1)S(1)}, bf16[256,1,128]{2,0,1:T(8,128)(2,1)S(1)}, u32[]{:S(2)}, u32[]{:S(2)}) collective-permute-start(bf16[256,1,128]{2,0,1:T(8,128)(2,1)S(1)} %fusion.115), channel_id=1, source_target_pairs={{0,4},{4,8},{8,12},{12,16},{16,20},{20,24},{24,28},{28,0},{1,5},{5... | collective-permute-start | bytes 196616 | tf_op jit(solution)/shard_map/while/body/eval_jaxpr/ppermute | solution.py:14
  109.4 9.2 %collective-permute-start.2 = (bf16[256,1,128]{2,0,1:T(8,128)(2,1)S(1)}, bf16[256,1,128]{2,0,1:T(8,128)(2,1)S(1)}, u32[]{:S(2)}, u32[]{:S(2)}) collective-permute-start(bf16[256,1,128]{2,0,1:T(8,128)(2,1)S(1)} %copy.135), channel_id=1, source_target_pairs={{0,4},{4,8},{8,12},{12,16},{16,20},{20,24},{24,28},{28,0},{1,5},{5... | collective-permute-start | bytes 196616 | tf_op jit(solution)/shard_map/while/body/eval_jaxpr/ppermute | solution.py:14
  109.5 9.1 %collective-permute-start.3 = (bf16[256,1,128]{2,0,1:T(8,128)(2,1)S(1)}, bf16[256,1,128]{2,0,1:T(8,128)(2,1)S(1)}, u32[]{:S(2)}, u32[]{:S(2)}) collective-permute-start(bf16[256,1,128]{2,0,1:T(8,128)(2,1)S(1)} %copy.136), channel_id=1, source_target_pairs={{0,4},{4,8},{8,12},{12,16},{16,20},{20,24},{24,28},{28,0},{1,5},{5... | collective-permute-start | bytes 196616 | tf_op jit(solution)/shard_map/while/body/eval_jaxpr/ppermute | solution.py:14
  112.3 5.5 %collective-permute-start.4 = (bf16[256,1,128]{2,0,1:T(8,128)(2,1)S(1)}, bf16[256,1,128]{2,0,1:T(8,128)(2,1)S(1)}, u32[]{:S(2)}, u32[]{:S(2)}) collective-permute-start(bf16[256,1,128]{2,0,1:T(8,128)(2,1)S(1)} %fusion.114), channel_id=1, source_target_pairs={{0,4},{4,8},{8,12},{12,16},{16,20},{20,24},{24,28},{28,0},{1,5},{5... | collective-permute-start | bytes 196616 | tf_op jit(solution)/shard_map/while/body/eval_jaxpr/ppermute | solution.py:14
  112.8 5.7 %collective-permute-start.5 = (bf16[256,1,128]{2,0,1:T(8,128)(2,1)S(1)}, bf16[256,1,128]{2,0,1:T(8,128)(2,1)S(1)}, u32[]{:S(2)}, u32[]{:S(2)}) collective-permute-start(bf16[256,1,128]{2,0,1:T(8,128)(2,1)S(1)} %fusion.115), channel_id=1, source_target_pairs={{0,4},{4,8},{8,12},{12,16},{16,20},{20,24},{24,28},{28,0},{1,5},{5... | collective-permute-start | bytes 196616 | tf_op jit(solution)/shard_map/while/body/eval_jaxpr/ppermute | solution.py:14
  118.6 9.2 %collective-permute-start.2 = (bf16[256,1,128]{2,0,1:T(8,128)(2,1)S(1)}, bf16[256,1,128]{2,0,1:T(8,128)(2,1)S(1)}, u32[]{:S(2)}, u32[]{:S(2)}) collective-permute-start(bf16[256,1,128]{2,0,1:T(8,128)(2,1)S(1)} %copy.135), channel_id=1, source_target_pairs={{0,4},{4,8},{8,12},{12,16},{16,20},{20,24},{24,28},{28,0},{1,5},{5... | collective-permute-start | bytes 196616 | tf_op jit(solution)/shard_map/while/body/eval_jaxpr/ppermute | solution.py:14
  118.7 9.1 %collective-permute-start.3 = (bf16[256,1,128]{2,0,1:T(8,128)(2,1)S(1)}, bf16[256,1,128]{2,0,1:T(8,128)(2,1)S(1)}, u32[]{:S(2)}, u32[]{:S(2)}) collective-permute-start(bf16[256,1,128]{2,0,1:T(8,128)(2,1)S(1)} %copy.136), channel_id=1, source_target_pairs={{0,4},{4,8},{8,12},{12,16},{16,20},{20,24},{24,28},{28,0},{1,5},{5... | collective-permute-start | bytes 196616 | tf_op jit(solution)/shard_map/while/body/eval_jaxpr/ppermute | solution.py:14
  121.5 5.5 %collective-permute-start.4 = (bf16[256,1,128]{2,0,1:T(8,128)(2,1)S(1)}, bf16[256,1,128]{2,0,1:T(8,128)(2,1)S(1)}, u32[]{:S(2)}, u32[]{:S(2)}) collective-permute-start(bf16[256,1,128]{2,0,1:T(8,128)(2,1)S(1)} %fusion.114), channel_id=1, source_target_pairs={{0,4},{4,8},{8,12},{12,16},{16,20},{20,24},{24,28},{28,0},{1,5},{5... | collective-permute-start | bytes 196616 | tf_op jit(solution)/shard_map/while/body/eval_jaxpr/ppermute | solution.py:14
  122.0 5.7 %collective-permute-start.5 = (bf16[256,1,128]{2,0,1:T(8,128)(2,1)S(1)}, bf16[256,1,128]{2,0,1:T(8,128)(2,1)S(1)}, u32[]{:S(2)}, u32[]{:S(2)}) collective-permute-start(bf16[256,1,128]{2,0,1:T(8,128)(2,1)S(1)} %fusion.115), channel_id=1, source_target_pairs={{0,4},{4,8},{8,12},{12,16},{16,20},{20,24},{24,28},{28,0},{1,5},{5... | collective-permute-start | bytes 196616 | tf_op jit(solution)/shard_map/while/body/eval_jaxpr/ppermute | solution.py:14
  127.8 9.2 %collective-permute-start.2 = (bf16[256,1,128]{2,0,1:T(8,128)(2,1)S(1)}, bf16[256,1,128]{2,0,1:T(8,128)(2,1)S(1)}, u32[]{:S(2)}, u32[]{:S(2)}) collective-permute-start(bf16[256,1,128]{2,0,1:T(8,128)(2,1)S(1)} %copy.135), channel_id=1, source_target_pairs={{0,4},{4,8},{8,12},{12,16},{16,20},{20,24},{24,28},{28,0},{1,5},{5... | collective-permute-start | bytes 196616 | tf_op jit(solution)/shard_map/while/body/eval_jaxpr/ppermute | solution.py:14
  127.9 9.1 %collective-permute-start.3 = (bf16[256,1,128]{2,0,1:T(8,128)(2,1)S(1)}, bf16[256,1,128]{2,0,1:T(8,128)(2,1)S(1)}, u32[]{:S(2)}, u32[]{:S(2)}) collective-permute-start(bf16[256,1,128]{2,0,1:T(8,128)(2,1)S(1)} %copy.136), channel_id=1, source_target_pairs={{0,4},{4,8},{8,12},{12,16},{16,20},{20,24},{24,28},{28,0},{1,5},{5... | collective-permute-start | bytes 196616 | tf_op jit(solution)/shard_map/while/body/eval_jaxpr/ppermute | solution.py:14
  131.2 5.7 %collective-permute-start.5 = (bf16[256,1,128]{2,0,1:T(8,128)(2,1)S(1)}, bf16[256,1,128]{2,0,1:T(8,128)(2,1)S(1)}, u32[]{:S(2)}, u32[]{:S(2)}) collective-permute-start(bf16[256,1,128]{2,0,1:T(8,128)(2,1)S(1)} %fusion.115), channel_id=1, source_target_pairs={{0,4},{4,8},{8,12},{12,16},{16,20},{20,24},{24,28},{28,0},{1,5},{5... | collective-permute-start | bytes 196616 | tf_op jit(solution)/shard_map/while/body/eval_jaxpr/ppermute | solution.py:14
  137.0 9.2 %collective-permute-start.2 = (bf16[256,1,128]{2,0,1:T(8,128)(2,1)S(1)}, bf16[256,1,128]{2,0,1:T(8,128)(2,1)S(1)}, u32[]{:S(2)}, u32[]{:S(2)}) collective-permute-start(bf16[256,1,128]{2,0,1:T(8,128)(2,1)S(1)} %copy.135), channel_id=1, source_target_pairs={{0,4},{4,8},{8,12},{12,16},{16,20},{20,24},{24,28},{28,0},{1,5},{5... | collective-permute-start | bytes 196616 | tf_op jit(solution)/shard_map/while/body/eval_jaxpr/ppermute | solution.py:14
  137.1 9.1 %collective-permute-start.3 = (bf16[256,1,128]{2,0,1:T(8,128)(2,1)S(1)}, bf16[256,1,128]{2,0,1:T(8,128)(2,1)S(1)}, u32[]{:S(2)}, u32[]{:S(2)}) collective-permute-start(bf16[256,1,128]{2,0,1:T(8,128)(2,1)S(1)} %copy.136), channel_id=1, source_target_pairs={{0,4},{4,8},{8,12},{12,16},{16,20},{20,24},{24,28},{28,0},{1,5},{5... | collective-permute-start | bytes 196616 | tf_op jit(solution)/shard_map/while/body/eval_jaxpr/ppermute | solution.py:14
  139.9 5.5 %collective-permute-start.4 = (bf16[256,1,128]{2,0,1:T(8,128)(2,1)S(1)}, bf16[256,1,128]{2,0,1:T(8,128)(2,1)S(1)}, u32[]{:S(2)}, u32[]{:S(2)}) collective-permute-start(bf16[256,1,128]{2,0,1:T(8,128)(2,1)S(1)} %fusion.114), channel_id=1, source_target_pairs={{0,4},{4,8},{8,12},{12,16},{16,20},{20,24},{24,28},{28,0},{1,5},{5... | collective-permute-start | bytes 196616 | tf_op jit(solution)/shard_map/while/body/eval_jaxpr/ppermute | solution.py:14
  140.4 5.7 %collective-permute-start.5 = (bf16[256,1,128]{2,0,1:T(8,128)(2,1)S(1)}, bf16[256,1,128]{2,0,1:T(8,128)(2,1)S(1)}, u32[]{:S(2)}, u32[]{:S(2)}) collective-permute-start(bf16[256,1,128]{2,0,1:T(8,128)(2,1)S(1)} %fusion.115), channel_id=1, source_target_pairs={{0,4},{4,8},{8,12},{12,16},{16,20},{20,24},{24,28},{28,0},{1,5},{5... | collective-permute-start | bytes 196616 | tf_op jit(solution)/shard_map/while/body/eval_jaxpr/ppermute | solution.py:14
  146.2 9.2 %collective-permute-start.2 = (bf16[256,1,128]{2,0,1:T(8,128)(2,1)S(1)}, bf16[256,1,128]{2,0,1:T(8,128)(2,1)S(1)}, u32[]{:S(2)}, u32[]{:S(2)}) collective-permute-start(bf16[256,1,128]{2,0,1:T(8,128)(2,1)S(1)} %copy.135), channel_id=1, source_target_pairs={{0,4},{4,8},{8,12},{12,16},{16,20},{20,24},{24,28},{28,0},{1,5},{5... | collective-permute-start | bytes 196616 | tf_op jit(solution)/shard_map/while/body/eval_jaxpr/ppermute | solution.py:14
  146.3 9.1 %collective-permute-start.3 = (bf16[256,1,128]{2,0,1:T(8,128)(2,1)S(1)}, bf16[256,1,128]{2,0,1:T(8,128)(2,1)S(1)}, u32[]{:S(2)}, u32[]{:S(2)}) collective-permute-start(bf16[256,1,128]{2,0,1:T(8,128)(2,1)S(1)} %copy.136), channel_id=1, source_target_pairs={{0,4},{4,8},{8,12},{12,16},{16,20},{20,24},{24,28},{28,0},{1,5},{5... | collective-permute-start | bytes 196616 | tf_op jit(solution)/shard_map/while/body/eval_jaxpr/ppermute | solution.py:14
  149.6 5.7 %collective-permute-start.5 = (bf16[256,1,128]{2,0,1:T(8,128)(2,1)S(1)}, bf16[256,1,128]{2,0,1:T(8,128)(2,1)S(1)}, u32[]{:S(2)}, u32[]{:S(2)}) collective-permute-start(bf16[256,1,128]{2,0,1:T(8,128)(2,1)S(1)} %fusion.115), channel_id=1, source_target_pairs={{0,4},{4,8},{8,12},{12,16},{16,20},{20,24},{24,28},{28,0},{1,5},{5... | collective-permute-start | bytes 196616 | tf_op jit(solution)/shard_map/while/body/eval_jaxpr/ppermute | solution.py:14
  155.4 9.2 %collective-permute-start.2 = (bf16[256,1,128]{2,0,1:T(8,128)(2,1)S(1)}, bf16[256,1,128]{2,0,1:T(8,128)(2,1)S(1)}, u32[]{:S(2)}, u32[]{:S(2)}) collective-permute-start(bf16[256,1,128]{2,0,1:T(8,128)(2,1)S(1)} %copy.135), channel_id=1, source_target_pairs={{0,4},{4,8},{8,12},{12,16},{16,20},{20,24},{24,28},{28,0},{1,5},{5... | collective-permute-start | bytes 196616 | tf_op jit(solution)/shard_map/while/body/eval_jaxpr/ppermute | solution.py:14
  155.5 9.1 %collective-permute-start.3 = (bf16[256,1,128]{2,0,1:T(8,128)(2,1)S(1)}, bf16[256,1,128]{2,0,1:T(8,128)(2,1)S(1)}, u32[]{:S(2)}, u32[]{:S(2)}) collective-permute-start(bf16[256,1,128]{2,0,1:T(8,128)(2,1)S(1)} %copy.136), channel_id=1, source_target_pairs={{0,4},{4,8},{8,12},{12,16},{16,20},{20,24},{24,28},{28,0},{1,5},{5... | collective-permute-start | bytes 196616 | tf_op jit(solution)/shard_map/while/body/eval_jaxpr/ppermute | solution.py:14
  158.3 5.5 %collective-permute-start.4 = (bf16[256,1,128]{2,0,1:T(8,128)(2,1)S(1)}, bf16[256,1,128]{2,0,1:T(8,128)(2,1)S(1)}, u32[]{:S(2)}, u32[]{:S(2)}) collective-permute-start(bf16[256,1,128]{2,0,1:T(8,128)(2,1)S(1)} %fusion.114), channel_id=1, source_target_pairs={{0,4},{4,8},{8,12},{12,16},{16,20},{20,24},{24,28},{28,0},{1,5},{5... | collective-permute-start | bytes 196616 | tf_op jit(solution)/shard_map/while/body/eval_jaxpr/ppermute | solution.py:14
  158.8 5.7 %collective-permute-start.5 = (bf16[256,1,128]{2,0,1:T(8,128)(2,1)S(1)}, bf16[256,1,128]{2,0,1:T(8,128)(2,1)S(1)}, u32[]{:S(2)}, u32[]{:S(2)}) collective-permute-start(bf16[256,1,128]{2,0,1:T(8,128)(2,1)S(1)} %fusion.115), channel_id=1, source_target_pairs={{0,4},{4,8},{8,12},{12,16},{16,20},{20,24},{24,28},{28,0},{1,5},{5... | collective-permute-start | bytes 196616 | tf_op jit(solution)/shard_map/while/body/eval_jaxpr/ppermute | solution.py:14
  166.4 8.1 %all-to-all-start.2 = ((bf16[4,2,4096]{2,1,0:T(2,128)(2,1)}), bf16[4,2,4096]{2,1,0:T(2,128)(2,1)S(1)}, u32[]{:S(2)}, u32[]{:S(2)}) async-start(bf16[4,2,4096]{2,1,0:T(2,128)(2,1)} %reshape.646), calls=%async_computation.2 | async-start | bytes 131072 | tf_op jit(solution)/shard_map/all_to_all | solution.py:159
  174.5 8.1 %all-to-all-start.3 = ((bf16[4,2,4096]{2,1,0:T(2,128)(2,1)}), bf16[4,2,4096]{2,1,0:T(2,128)(2,1)S(1)}, u32[]{:S(2)}, u32[]{:S(2)}) async-start(bf16[4,2,4096]{2,1,0:T(2,128)(2,1)} %reshape.648), calls=%async_computation.3 | async-start | bytes 131072 | tf_op jit(solution)/shard_map/all_to_all | solution.py:160
  (14 other events, 80.7 us)
where the time goes:
time: 185 us; the launch traced here: 183 us
  waiting for transfers between devices  43.8 us (24%)
  other arithmetic  43.5 us (24%)
  matrix products  38.5 us (21%)
  starting transfers between devices  33.8 us (18%)
  local copies, waits for them, and re-layouts  21 us (11%)
    ppermute x46, waiting for transfers between devices, from_behind(): return lax.ppermute(value, axis, pairs)  34.9 us
    ppermute x46, starting transfers between devices, from_behind(): return lax.ppermute(value, axis, pairs)  18.8 us
    dot_general x16, matrix products, block_scores(): jnp.einsum('tngd,knd->tngk', query_block, key_block, preferred_element_ty...  13.9 us
    unnamed x39, local copies, waits for them, and re-layouts  10.8 us
    le x15, other arithmetic, block_mask(): key_pos[None, :] <= query_pos[:, None]  9.68 us
    while x37, local copies, waits for them, and re-layouts  8.95 us
    reduce_sum x16, other arithmetic, row_info(): jnp.sum((shard_tiles[:, None] >= doc_ends[None, :]).astype(jnp.int32), ax...  7.69 us
    dot_general x8, matrix products, forward_block(): jnp.einsum('tngk,knd->tngd', weights.astype(jnp.bfloat16), value_block, p...  7.21 us
  transfers between devices with their start and end apart: 50, of which 27 were waited for; matrix products, arithmetic and copies ran while one was open for 43% of the time, Pallas kernels for 0%

commit v1 on v0

--- a/solution.py
+++ b/solution.py
@@ -71,7 +71,12 @@
 def body(queries, key_proj, value_proj, out_grad, tile_order, doc_tiles):
     key_rows, value_rows = (
         lax.all_to_all(key_proj, "head", split_axis=1, concat_axis=0, tiled=True),
-        lax.all_to_all(value_proj, "head", split_axis=1, concat_axis=0, tiled=True),
+        jnp.concatenate(
+            lax.all_to_all(
+                jnp.stack(jnp.split(value_proj, lax.axis_size("head"), axis=1)), "head", 0, 0
+            ),
+            axis=0,
+        ),
     )
     row_count = queries.shape[0]
     kv_local = key_rows.shape[1]

time: 185 us -> 205 us (1.11)
  other arithmetic: 43.5 us -> 60.6 us
    le x15, other arithmetic: 9.68 us -> 15.1 us  [block_mask(): key_pos[None, :] <= query_pos[:, None]]
    mul x16, other arithmetic: 6.43 us -> 11.7 us  [row_info(): positions = (shard_tiles[:, None] * tile_len + offsets[None, :]).reshape(-1)]
    reduce_sum x16, other arithmetic: 7.69 us -> 12 us  [row_info(): jnp.sum((shard_tiles[:, None] >= doc_ends[None, :]).astype(jnp.int32), ax...]
    unnamed x39 -> x35, local copies, waits for them, and re-layouts: 10.8 us -> 9.38 us
  transfers between devices with their start and end apart: 50 -> 50, of which waited for: 27 -> 27; matrix products, arithmetic and copies ran while one was open for 43% -> 47% of each run, Pallas kernels for 0% -> 0%
where the time goes in v1:
time: 205 us; the launch traced here: 203 us
  other arithmetic  60.6 us (30%)
  waiting for transfers between devices  45.3 us (22%)
  matrix products  40.2 us (20%)
  starting transfers between devices  33.3 us (16%)
  local copies, waits for them, and re-layouts  20.8 us (10%)
    ppermute x46, waiting for transfers between devices, from_behind(): return lax.ppermute(value, axis, pairs)  35.8 us
    ppermute x46, starting transfers between devices, from_behind(): return lax.ppermute(value, axis, pairs)  18.3 us
    le x15, other arithmetic, block_mask(): key_pos[None, :] <= query_pos[:, None]  15.1 us
    dot_general x16, matrix products, block_scores(): jnp.einsum('tngd,knd->tngk', query_block, key_block, preferred_element_ty...  14.9 us
    reduce_sum x16, other arithmetic, row_info(): jnp.sum((shard_tiles[:, None] >= doc_ends[None, :]).astype(jnp.int32), ax...  12 us
    mul x16, other arithmetic, row_info(): positions = (shard_tiles[:, None] * tile_len + offsets[None, :]).reshape(-1)  11.7 us
    unnamed x35, local copies, waits for them, and re-layouts  9.38 us
    while x37, local copies, waits for them, and re-layouts  8.96 us
  transfers between devices with their start and end apart: 50, of which 27 were waited for; matrix products, arithmetic and copies ran while one was open for 47% of the time, Pallas kernels for 0%

profile of v1, /device:TPU:0, one launch (start us, length us, event | category | flops | bytes accessed | tf_op | source)
XLA Modules:
  0.0 202.9 jit_solution(906296815873927551)
XLA Ops:
  0.7 1.6 copy.91
  2.2 5.2 %all-to-all-start = ((bf16[64,4,128]{2,0,1:T(8,128)(2,1)}), bf16[64,4,128]{2,0,1:T(8,128)(2,1)S(1)}, u32[]{:S(2)}, u32[]{:S(2)}) async-start(bf16[64,4,128]{2,0,1:T(8,128)(2,1)} %copy.91), calls=%async_computation | async-start | bytes 131072 | tf_op jit(solution)/shard_map/all_to_all | solution.py:73
  12.2 3.3 %all-to-all-start.1 = ((bf16[4,64,1,128]{3,1,2,0:T(8,128)(2,1)}), bf16[4,64,1,128]{3,1,2,0:T(8,128)(2,1)S(1)}, u32[]{:S(2)}, u32[]{:S(2)}) async-start(bf16[4,64,1,128]{3,1,2,0:T(8,128)(2,1)} %pad_maximum_fusion), calls=%async_computation.1 | async-start | bytes 131072 | tf_op jit(solution)/shard_map/all_to_all | solution.py:75
  18.2 2.2 %all-to-all-done.1 = bf16[4,64,1,128]{3,1,2,0:T(8,128)(2,1)S(1)} async-done(((bf16[4,64,1,128]{3,1,2,0:T(8,128)(2,1)}), bf16[4,64,1,128]{3,1,2,0:T(8,128)(2,1)S(1)}, u32[]{:S(2)}, u32[]{:S(2)}) %all-to-all-start.1) | async-done | bytes 65568 | tf_op jit(solution)/shard_map/all_to_all | solution.py:75
  21.0 1.4 fusion.46
  22.4 1.3 fusion.50
  23.7 1.5 fusion.52
  25.3 1.5 copy.100
  26.8 62.3 %while.48 = (s32[]{:T(128)}, bf16[256,1,128]{2,0,1:T(8,128)(2,1)}, bf16[256,1,128]{2,0,1:T(8,128)(2,1)}, f32[256,1,8]{0,2,1:T(8,128)S(1)}, f32[256,1,8]{0,2,1:T(...) while((s32[]{:T(128)}, bf16[256,1,128]{2,0,1:T(8,128)(2,1)}, ...), condition=%wide.region_8.9_spmd.clone, body=%wide.region_4.0_spmd.clone.sunk | while | flops 274930240 | bytes 10232312 | solution.py:125
  26.9 1.7 collective-permute-start.1
  28.6 1.3 add_bitcast_fusion.9
  35.8 1.4 collective-permute-start.1
  37.2 1.3 add_bitcast_fusion.9
  45.9 1.3 add_bitcast_fusion.9
  53.7 1.3 add_bitcast_fusion.9
  57.5 1.9 collective-permute-done
  62.6 1.3 add_bitcast_fusion.9
  66.4 1.9 collective-permute-done
  71.5 1.3 add_bitcast_fusion.9
  75.3 1.9 collective-permute-done
  80.4 1.3 add_bitcast_fusion.9
  84.2 1.9 collective-permute-done
  90.6 3.3 %multiply_reduce_fusion = (f32[256,8]{1,0:T(8,128)}, bf16[256,1,8,128]{3,2,0,1:T(8,128)(2,1)}) fusion(bf16[256,8,128]{2,1,0:T(8,128)(2,1)} %param.13, f32[256,8]{1,0:T(8,128)} %copy.101, f32[256,1,8,128]{3,0,2,1:T(8,128)S(1)} %get-tuple-element.648), kind=kLoop, calls=%fused_computation.83 | loop fusion | flops 1570816 | bytes 2113536 | tf_op jit(solution)/shard_map/reduce_sum | solution.py:129
  94.9 89.1 %while.49 = (s32[]{:T(128)}, bf16[256,1,128]{2,0,1:T(8,128)(2,1)S(1)}, bf16[256,1,128]{2,0,1:T(8,128)(2,1)S(1)}, f32[256,1,128]{2,0,1:T(8,128)S(1)}, f32[256,1,1...) while((s32[]{:T(128)}, ...), condition=%wide.region_12.13_spmd.clone, body=%wide.region_10.12_spmd.clone.sunk | while | flops 675742272 | bytes 16081516 | solution.py:151
  97.6 1.3 bitcast_select_fusion.4
  100.3 1.4 collective-permute-start.5
  102.6 2.7 %collective-permute-done.4 = bf16[256,1,128]{2,0,1:T(8,128)(2,1)S(1)} collective-permute-done((bf16[256,1,128]{2,0,1:T(8,128)(2,1)S(1)}, bf16[256,1,128]{2,0,1:T(8,128)(2,1)S(1)}, u32[]{:S(2)}, u32[]{:S(2)}) %collective-permute-start.4) | collective-permute-done | bytes 65568 | tf_op jit(solution)/shard_map/while/body/eval_jaxpr/ppermute | solution.py:14
  108.7 1.3 bitcast_select_fusion.4
  111.4 1.5 collective-permute-start.5
  113.8 2.7 %collective-permute-done.4 = bf16[256,1,128]{2,0,1:T(8,128)(2,1)S(1)} collective-permute-done((bf16[256,1,128]{2,0,1:T(8,128)(2,1)S(1)}, bf16[256,1,128]{2,0,1:T(8,128)(2,1)S(1)}, u32[]{:S(2)}, u32[]{:S(2)}) %collective-permute-start.4) | collective-permute-done | bytes 65568 | tf_op jit(solution)/shard_map/while/body/eval_jaxpr/ppermute | solution.py:14
  119.9 1.3 bitcast_select_fusion.4
  122.5 1.5 collective-permute-start.5
  124.9 2.6 %collective-permute-done.4 = bf16[256,1,128]{2,0,1:T(8,128)(2,1)S(1)} collective-permute-done((bf16[256,1,128]{2,0,1:T(8,128)(2,1)S(1)}, bf16[256,1,128]{2,0,1:T(8,128)(2,1)S(1)}, u32[]{:S(2)}, u32[]{:S(2)}) %collective-permute-start.4) | collective-permute-done | bytes 65568 | tf_op jit(solution)/shard_map/while/body/eval_jaxpr/ppermute | solution.py:14
  133.7 1.5 collective-permute-start.5
  136.1 2.6 %collective-permute-done.4 = bf16[256,1,128]{2,0,1:T(8,128)(2,1)S(1)} collective-permute-done((bf16[256,1,128]{2,0,1:T(8,128)(2,1)S(1)}, bf16[256,1,128]{2,0,1:T(8,128)(2,1)S(1)}, u32[]{:S(2)}, u32[]{:S(2)}) %collective-permute-start.4) | collective-permute-done | bytes 65568 | tf_op jit(solution)/shard_map/while/body/eval_jaxpr/ppermute | solution.py:14
  144.8 1.5 collective-permute-start.5
  147.2 2.6 %collective-permute-done.4 = bf16[256,1,128]{2,0,1:T(8,128)(2,1)S(1)} collective-permute-done((bf16[256,1,128]{2,0,1:T(8,128)(2,1)S(1)}, bf16[256,1,128]{2,0,1:T(8,128)(2,1)S(1)}, u32[]{:S(2)}, u32[]{:S(2)}) %collective-permute-start.4) | collective-permute-done | bytes 65568 | tf_op jit(solution)/shard_map/while/body/eval_jaxpr/ppermute | solution.py:14
  156.0 1.5 collective-permute-start.5
  158.4 2.6 %collective-permute-done.4 = bf16[256,1,128]{2,0,1:T(8,128)(2,1)S(1)} collective-permute-done((bf16[256,1,128]{2,0,1:T(8,128)(2,1)S(1)}, bf16[256,1,128]{2,0,1:T(8,128)(2,1)S(1)}, u32[]{:S(2)}, u32[]{:S(2)}) %collective-permute-start.4) | collective-permute-done | bytes 65568 | tf_op jit(solution)/shard_map/while/body/eval_jaxpr/ppermute | solution.py:14
  167.1 1.5 collective-permute-start.5
  169.5 2.6 %collective-permute-done.4 = bf16[256,1,128]{2,0,1:T(8,128)(2,1)S(1)} collective-permute-done((bf16[256,1,128]{2,0,1:T(8,128)(2,1)S(1)}, bf16[256,1,128]{2,0,1:T(8,128)(2,1)S(1)}, u32[]{:S(2)}, u32[]{:S(2)}) %collective-permute-start.4) | collective-permute-done | bytes 65568 | tf_op jit(solution)/shard_map/while/body/eval_jaxpr/ppermute | solution.py:14
  178.3 1.5 collective-permute-start.5
  180.7 2.6 %collective-permute-done.4 = bf16[256,1,128]{2,0,1:T(8,128)(2,1)S(1)} collective-permute-done((bf16[256,1,128]{2,0,1:T(8,128)(2,1)S(1)}, bf16[256,1,128]{2,0,1:T(8,128)(2,1)S(1)}, u32[]{:S(2)}, u32[]{:S(2)}) %collective-permute-start.4) | collective-permute-done | bytes 65568 | tf_op jit(solution)/shard_map/while/body/eval_jaxpr/ppermute | solution.py:14
  185.9 3.3 %all-to-all-start.2 = ((bf16[4,2,4096]{2,1,0:T(2,128)(2,1)}), bf16[4,2,4096]{2,1,0:T(2,128)(2,1)S(1)}, u32[]{:S(2)}, u32[]{:S(2)}) async-start(bf16[4,2,4096]{2,1,0:T(2,128)(2,1)} %reshape.650), calls=%async_computation.2 | async-start | bytes 131072 | tf_op jit(solution)/shard_map/all_to_all | solution.py:164
  190.5 3.5 %all-to-all-done.2 = bf16[4,2,4096]{2,1,0:T(2,128)(2,1)S(1)} async-done(((bf16[4,2,4096]{2,1,0:T(2,128)(2,1)}), bf16[4,2,4096]{2,1,0:T(2,128)(2,1)S(1)}, u32[]{:S(2)}, u32[]{:S(2)}) %all-to-all-start.2) | async-done | bytes 65568 | tf_op jit(solution)/shard_map/all_to_all | solution.py:164
  194.0 3.3 %all-to-all-start.3 = ((bf16[4,2,4096]{2,1,0:T(2,128)(2,1)}), bf16[4,2,4096]{2,1,0:T(2,128)(2,1)S(1)}, u32[]{:S(2)}, u32[]{:S(2)}) async-start(bf16[4,2,4096]{2,1,0:T(2,128)(2,1)} %reshape.652), calls=%async_computation.3 | async-start | bytes 131072 | tf_op jit(solution)/shard_map/all_to_all | solution.py:165
  197.3 1.5 fusion.61
  199.5 2.6 %all-to-all-done.3 = bf16[4,2,4096]{2,1,0:T(2,128)(2,1)S(1)} async-done(((bf16[4,2,4096]{2,1,0:T(2,128)(2,1)}), bf16[4,2,4096]{2,1,0:T(2,128)(2,1)S(1)}, u32[]{:S(2)}, u32[]{:S(2)}) %all-to-all-start.3) | async-done | bytes 65568 | tf_op jit(solution)/shard_map/all_to_all | solution.py:165
  (318 shorter events, 108.0 us)
Async XLA Ops:
  2.2 10.0 %all-to-all-start = ((bf16[64,4,128]{2,0,1:T(8,128)(2,1)}), bf16[64,4,128]{2,0,1:T(8,128)(2,1)S(1)}, u32[]{:S(2)}, u32[]{:S(2)}) async-start(bf16[64,4,128]{2,0,1:T(8,128)(2,1)} %copy.91), calls=%async_computation | async-start | bytes 131072 | tf_op jit(solution)/shard_map/all_to_all | solution.py:73
  12.2 8.1 %all-to-all-start.1 = ((bf16[4,64,1,128]{3,1,2,0:T(8,128)(2,1)}), bf16[4,64,1,128]{3,1,2,0:T(8,128)(2,1)S(1)}, u32[]{:S(2)}, u32[]{:S(2)}) async-start(bf16[4,64,1,128]{3,1,2,0:T(8,128)(2,1)} %pad_maximum_fusion), calls=%async_computation.1 | async-start | bytes 131072 | tf_op jit(solution)/shard_map/all_to_all | solution.py:75
  26.9 5.8 %collective-permute-start = (bf16[256,1,128]{2,0,1:T(8,128)(2,1)}, bf16[256,1,128]{2,0,1:T(8,128)(2,1)S(1)}, u32[]{:S(2)}, u32[]{:S(2)}) collective-permute-start(bf16[256,1,128]{2,0,1:T(8,128)(2,1)} %get-tuple-element.1192), channel_id=1, source_target_pairs={{0,4},{4,8},{8,12},{12,16},{16,20},{20,24},{24,28},{28,0},{1,5},{5... | collective-permute-start | bytes 196616 | tf_op jit(solution)/shard_map/while/body/eval_jaxpr/ppermute | solution.py:14
  26.9 7.3 %collective-permute-start.1 = (bf16[256,1,128]{2,0,1:T(8,128)(2,1)}, bf16[256,1,128]{2,0,1:T(8,128)(2,1)S(1)}, u32[]{:S(2)}, u32[]{:S(2)}) collective-permute-start(bf16[256,1,128]{2,0,1:T(8,128)(2,1)} %get-tuple-element.1193), channel_id=1, source_target_pairs={{0,4},{4,8},{8,12},{12,16},{16,20},{20,24},{24,28},{28,0},{1,5},{5... | collective-permute-start | bytes 196616 | tf_op jit(solution)/shard_map/while/body/eval_jaxpr/ppermute | solution.py:14
  35.8 5.8 %collective-permute-start = (bf16[256,1,128]{2,0,1:T(8,128)(2,1)}, bf16[256,1,128]{2,0,1:T(8,128)(2,1)S(1)}, u32[]{:S(2)}, u32[]{:S(2)}) collective-permute-start(bf16[256,1,128]{2,0,1:T(8,128)(2,1)} %get-tuple-element.1192), channel_id=1, source_target_pairs={{0,4},{4,8},{8,12},{12,16},{16,20},{20,24},{24,28},{28,0},{1,5},{5... | collective-permute-start | bytes 196616 | tf_op jit(solution)/shard_map/while/body/eval_jaxpr/ppermute | solution.py:14
  35.8 7.3 %collective-permute-start.1 = (bf16[256,1,128]{2,0,1:T(8,128)(2,1)}, bf16[256,1,128]{2,0,1:T(8,128)(2,1)S(1)}, u32[]{:S(2)}, u32[]{:S(2)}) collective-permute-start(bf16[256,1,128]{2,0,1:T(8,128)(2,1)} %get-tuple-element.1193), channel_id=1, source_target_pairs={{0,4},{4,8},{8,12},{12,16},{16,20},{20,24},{24,28},{28,0},{1,5},{5... | collective-permute-start | bytes 196616 | tf_op jit(solution)/shard_map/while/body/eval_jaxpr/ppermute | solution.py:14
  44.7 5.8 %collective-permute-start = (bf16[256,1,128]{2,0,1:T(8,128)(2,1)}, bf16[256,1,128]{2,0,1:T(8,128)(2,1)S(1)}, u32[]{:S(2)}, u32[]{:S(2)}) collective-permute-start(bf16[256,1,128]{2,0,1:T(8,128)(2,1)} %get-tuple-element.1192), channel_id=1, source_target_pairs={{0,4},{4,8},{8,12},{12,16},{16,20},{20,24},{24,28},{28,0},{1,5},{5... | collective-permute-start | bytes 196616 | tf_op jit(solution)/shard_map/while/body/eval_jaxpr/ppermute | solution.py:14
  44.7 7.3 %collective-permute-start.1 = (bf16[256,1,128]{2,0,1:T(8,128)(2,1)}, bf16[256,1,128]{2,0,1:T(8,128)(2,1)S(1)}, u32[]{:S(2)}, u32[]{:S(2)}) collective-permute-start(bf16[256,1,128]{2,0,1:T(8,128)(2,1)} %get-tuple-element.1193), channel_id=1, source_target_pairs={{0,4},{4,8},{8,12},{12,16},{16,20},{20,24},{24,28},{28,0},{1,5},{5... | collective-permute-start | bytes 196616 | tf_op jit(solution)/shard_map/while/body/eval_jaxpr/ppermute | solution.py:14
  53.6 5.8 %collective-permute-start = (bf16[256,1,128]{2,0,1:T(8,128)(2,1)}, bf16[256,1,128]{2,0,1:T(8,128)(2,1)S(1)}, u32[]{:S(2)}, u32[]{:S(2)}) collective-permute-start(bf16[256,1,128]{2,0,1:T(8,128)(2,1)} %get-tuple-element.1192), channel_id=1, source_target_pairs={{0,4},{4,8},{8,12},{12,16},{16,20},{20,24},{24,28},{28,0},{1,5},{5... | collective-permute-start | bytes 196616 | tf_op jit(solution)/shard_map/while/body/eval_jaxpr/ppermute | solution.py:14
  53.6 7.3 %collective-permute-start.1 = (bf16[256,1,128]{2,0,1:T(8,128)(2,1)}, bf16[256,1,128]{2,0,1:T(8,128)(2,1)S(1)}, u32[]{:S(2)}, u32[]{:S(2)}) collective-permute-start(bf16[256,1,128]{2,0,1:T(8,128)(2,1)} %get-tuple-element.1193), channel_id=1, source_target_pairs={{0,4},{4,8},{8,12},{12,16},{16,20},{20,24},{24,28},{28,0},{1,5},{5... | collective-permute-start | bytes 196616 | tf_op jit(solution)/shard_map/while/body/eval_jaxpr/ppermute | solution.py:14
  62.5 5.8 %collective-permute-start = (bf16[256,1,128]{2,0,1:T(8,128)(2,1)}, bf16[256,1,128]{2,0,1:T(8,128)(2,1)S(1)}, u32[]{:S(2)}, u32[]{:S(2)}) collective-permute-start(bf16[256,1,128]{2,0,1:T(8,128)(2,1)} %get-tuple-element.1192), channel_id=1, source_target_pairs={{0,4},{4,8},{8,12},{12,16},{16,20},{20,24},{24,28},{28,0},{1,5},{5... | collective-permute-start | bytes 196616 | tf_op jit(solution)/shard_map/while/body/eval_jaxpr/ppermute | solution.py:14
  62.5 7.3 %collective-permute-start.1 = (bf16[256,1,128]{2,0,1:T(8,128)(2,1)}, bf16[256,1,128]{2,0,1:T(8,128)(2,1)S(1)}, u32[]{:S(2)}, u32[]{:S(2)}) collective-permute-start(bf16[256,1,128]{2,0,1:T(8,128)(2,1)} %get-tuple-element.1193), channel_id=1, source_target_pairs={{0,4},{4,8},{8,12},{12,16},{16,20},{20,24},{24,28},{28,0},{1,5},{5... | collective-permute-start | bytes 196616 | tf_op jit(solution)/shard_map/while/body/eval_jaxpr/ppermute | solution.py:14
  71.4 5.8 %collective-permute-start = (bf16[256,1,128]{2,0,1:T(8,128)(2,1)}, bf16[256,1,128]{2,0,1:T(8,128)(2,1)S(1)}, u32[]{:S(2)}, u32[]{:S(2)}) collective-permute-start(bf16[256,1,128]{2,0,1:T(8,128)(2,1)} %get-tuple-element.1192), channel_id=1, source_target_pairs={{0,4},{4,8},{8,12},{12,16},{16,20},{20,24},{24,28},{28,0},{1,5},{5... | collective-permute-start | bytes 196616 | tf_op jit(solution)/shard_map/while/body/eval_jaxpr/ppermute | solution.py:14
  71.5 7.3 %collective-permute-start.1 = (bf16[256,1,128]{2,0,1:T(8,128)(2,1)}, bf16[256,1,128]{2,0,1:T(8,128)(2,1)S(1)}, u32[]{:S(2)}, u32[]{:S(2)}) collective-permute-start(bf16[256,1,128]{2,0,1:T(8,128)(2,1)} %get-tuple-element.1193), channel_id=1, source_target_pairs={{0,4},{4,8},{8,12},{12,16},{16,20},{20,24},{24,28},{28,0},{1,5},{5... | collective-permute-start | bytes 196616 | tf_op jit(solution)/shard_map/while/body/eval_jaxpr/ppermute | solution.py:14
  80.3 5.8 %collective-permute-start = (bf16[256,1,128]{2,0,1:T(8,128)(2,1)}, bf16[256,1,128]{2,0,1:T(8,128)(2,1)S(1)}, u32[]{:S(2)}, u32[]{:S(2)}) collective-permute-start(bf16[256,1,128]{2,0,1:T(8,128)(2,1)} %get-tuple-element.1192), channel_id=1, source_target_pairs={{0,4},{4,8},{8,12},{12,16},{16,20},{20,24},{24,28},{28,0},{1,5},{5... | collective-permute-start | bytes 196616 | tf_op jit(solution)/shard_map/while/body/eval_jaxpr/ppermute | solution.py:14
  80.4 7.3 %collective-permute-start.1 = (bf16[256,1,128]{2,0,1:T(8,128)(2,1)}, bf16[256,1,128]{2,0,1:T(8,128)(2,1)S(1)}, u32[]{:S(2)}, u32[]{:S(2)}) collective-permute-start(bf16[256,1,128]{2,0,1:T(8,128)(2,1)} %get-tuple-element.1193), channel_id=1, source_target_pairs={{0,4},{4,8},{8,12},{12,16},{16,20},{20,24},{24,28},{28,0},{1,5},{5... | collective-permute-start | bytes 196616 | tf_op jit(solution)/shard_map/while/body/eval_jaxpr/ppermute | solution.py:14
  94.9 11.1 %collective-permute-start.2 = (bf16[256,1,128]{2,0,1:T(8,128)(2,1)S(1)}, bf16[256,1,128]{2,0,1:T(8,128)(2,1)S(1)}, u32[]{:S(2)}, u32[]{:S(2)}) collective-permute-start(bf16[256,1,128]{2,0,1:T(8,128)(2,1)S(1)} %copy.167), channel_id=1, source_target_pairs={{0,4},{4,8},{8,12},{12,16},{16,20},{20,24},{24,28},{28,0},{1,5},{5... | collective-permute-start | bytes 196616 | tf_op jit(solution)/shard_map/while/body/eval_jaxpr/ppermute | solution.py:14
  95.0 11.0 %collective-permute-start.3 = (bf16[256,1,128]{2,0,1:T(8,128)(2,1)S(1)}, bf16[256,1,128]{2,0,1:T(8,128)(2,1)S(1)}, u32[]{:S(2)}, u32[]{:S(2)}) collective-permute-start(bf16[256,1,128]{2,0,1:T(8,128)(2,1)S(1)} %copy.168), channel_id=1, source_target_pairs={{0,4},{4,8},{8,12},{12,16},{16,20},{20,24},{24,28},{28,0},{1,5},{5... | collective-permute-start | bytes 196616 | tf_op jit(solution)/shard_map/while/body/eval_jaxpr/ppermute | solution.py:14
  99.7 5.5 %collective-permute-start.4 = (bf16[256,1,128]{2,0,1:T(8,128)(2,1)S(1)}, bf16[256,1,128]{2,0,1:T(8,128)(2,1)S(1)}, u32[]{:S(2)}, u32[]{:S(2)}) collective-permute-start(bf16[256,1,128]{2,0,1:T(8,128)(2,1)S(1)} %fusion.115), channel_id=1, source_target_pairs={{0,4},{4,8},{8,12},{12,16},{16,20},{20,24},{24,28},{28,0},{1,5},{5... | collective-permute-start | bytes 196616 | tf_op jit(solution)/shard_map/while/body/eval_jaxpr/ppermute | solution.py:14
  100.3 5.7 %collective-permute-start.5 = (bf16[256,1,128]{2,0,1:T(8,128)(2,1)S(1)}, bf16[256,1,128]{2,0,1:T(8,128)(2,1)S(1)}, u32[]{:S(2)}, u32[]{:S(2)}) collective-permute-start(bf16[256,1,128]{2,0,1:T(8,128)(2,1)S(1)} %fusion.116), channel_id=1, source_target_pairs={{0,4},{4,8},{8,12},{12,16},{16,20},{20,24},{24,28},{28,0},{1,5},{5... | collective-permute-start | bytes 196616 | tf_op jit(solution)/shard_map/while/body/eval_jaxpr/ppermute | solution.py:14
  106.1 11.1 %collective-permute-start.2 = (bf16[256,1,128]{2,0,1:T(8,128)(2,1)S(1)}, bf16[256,1,128]{2,0,1:T(8,128)(2,1)S(1)}, u32[]{:S(2)}, u32[]{:S(2)}) collective-permute-start(bf16[256,1,128]{2,0,1:T(8,128)(2,1)S(1)} %copy.167), channel_id=1, source_target_pairs={{0,4},{4,8},{8,12},{12,16},{16,20},{20,24},{24,28},{28,0},{1,5},{5... | collective-permute-start | bytes 196616 | tf_op jit(solution)/shard_map/while/body/eval_jaxpr/ppermute | solution.py:14
  106.1 11.0 %collective-permute-start.3 = (bf16[256,1,128]{2,0,1:T(8,128)(2,1)S(1)}, bf16[256,1,128]{2,0,1:T(8,128)(2,1)S(1)}, u32[]{:S(2)}, u32[]{:S(2)}) collective-permute-start(bf16[256,1,128]{2,0,1:T(8,128)(2,1)S(1)} %copy.168), channel_id=1, source_target_pairs={{0,4},{4,8},{8,12},{12,16},{16,20},{20,24},{24,28},{28,0},{1,5},{5... | collective-permute-start | bytes 196616 | tf_op jit(solution)/shard_map/while/body/eval_jaxpr/ppermute | solution.py:14
  110.9 5.5 %collective-permute-start.4 = (bf16[256,1,128]{2,0,1:T(8,128)(2,1)S(1)}, bf16[256,1,128]{2,0,1:T(8,128)(2,1)S(1)}, u32[]{:S(2)}, u32[]{:S(2)}) collective-permute-start(bf16[256,1,128]{2,0,1:T(8,128)(2,1)S(1)} %fusion.115), channel_id=1, source_target_pairs={{0,4},{4,8},{8,12},{12,16},{16,20},{20,24},{24,28},{28,0},{1,5},{5... | collective-permute-start | bytes 196616 | tf_op jit(solution)/shard_map/while/body/eval_jaxpr/ppermute | solution.py:14
  111.4 5.7 %collective-permute-start.5 = (bf16[256,1,128]{2,0,1:T(8,128)(2,1)S(1)}, bf16[256,1,128]{2,0,1:T(8,128)(2,1)S(1)}, u32[]{:S(2)}, u32[]{:S(2)}) collective-permute-start(bf16[256,1,128]{2,0,1:T(8,128)(2,1)S(1)} %fusion.116), channel_id=1, source_target_pairs={{0,4},{4,8},{8,12},{12,16},{16,20},{20,24},{24,28},{28,0},{1,5},{5... | collective-permute-start | bytes 196616 | tf_op jit(solution)/shard_map/while/body/eval_jaxpr/ppermute | solution.py:14
  117.2 11.1 %collective-permute-start.2 = (bf16[256,1,128]{2,0,1:T(8,128)(2,1)S(1)}, bf16[256,1,128]{2,0,1:T(8,128)(2,1)S(1)}, u32[]{:S(2)}, u32[]{:S(2)}) collective-permute-start(bf16[256,1,128]{2,0,1:T(8,128)(2,1)S(1)} %copy.167), channel_id=1, source_target_pairs={{0,4},{4,8},{8,12},{12,16},{16,20},{20,24},{24,28},{28,0},{1,5},{5... | collective-permute-start | bytes 196616 | tf_op jit(solution)/shard_map/while/body/eval_jaxpr/ppermute | solution.py:14
  117.3 11.0 %collective-permute-start.3 = (bf16[256,1,128]{2,0,1:T(8,128)(2,1)S(1)}, bf16[256,1,128]{2,0,1:T(8,128)(2,1)S(1)}, u32[]{:S(2)}, u32[]{:S(2)}) collective-permute-start(bf16[256,1,128]{2,0,1:T(8,128)(2,1)S(1)} %copy.168), channel_id=1, source_target_pairs={{0,4},{4,8},{8,12},{12,16},{16,20},{20,24},{24,28},{28,0},{1,5},{5... | collective-permute-start | bytes 196616 | tf_op jit(solution)/shard_map/while/body/eval_jaxpr/ppermute | solution.py:14
  122.5 5.7 %collective-permute-start.5 = (bf16[256,1,128]{2,0,1:T(8,128)(2,1)S(1)}, bf16[256,1,128]{2,0,1:T(8,128)(2,1)S(1)}, u32[]{:S(2)}, u32[]{:S(2)}) collective-permute-start(bf16[256,1,128]{2,0,1:T(8,128)(2,1)S(1)} %fusion.116), channel_id=1, source_target_pairs={{0,4},{4,8},{8,12},{12,16},{16,20},{20,24},{24,28},{28,0},{1,5},{5... | collective-permute-start | bytes 196616 | tf_op jit(solution)/shard_map/while/body/eval_jaxpr/ppermute | solution.py:14
  128.3 11.1 %collective-permute-start.2 = (bf16[256,1,128]{2,0,1:T(8,128)(2,1)S(1)}, bf16[256,1,128]{2,0,1:T(8,128)(2,1)S(1)}, u32[]{:S(2)}, u32[]{:S(2)}) collective-permute-start(bf16[256,1,128]{2,0,1:T(8,128)(2,1)S(1)} %copy.167), channel_id=1, source_target_pairs={{0,4},{4,8},{8,12},{12,16},{16,20},{20,24},{24,28},{28,0},{1,5},{5... | collective-permute-start | bytes 196616 | tf_op jit(solution)/shard_map/while/body/eval_jaxpr/ppermute | solution.py:14
  128.4 11.0 %collective-permute-start.3 = (bf16[256,1,128]{2,0,1:T(8,128)(2,1)S(1)}, bf16[256,1,128]{2,0,1:T(8,128)(2,1)S(1)}, u32[]{:S(2)}, u32[]{:S(2)}) collective-permute-start(bf16[256,1,128]{2,0,1:T(8,128)(2,1)S(1)} %copy.168), channel_id=1, source_target_pairs={{0,4},{4,8},{8,12},{12,16},{16,20},{20,24},{24,28},{28,0},{1,5},{5... | collective-permute-start | bytes 196616 | tf_op jit(solution)/shard_map/while/body/eval_jaxpr/ppermute | solution.py:14
  133.2 5.5 %collective-permute-start.4 = (bf16[256,1,128]{2,0,1:T(8,128)(2,1)S(1)}, bf16[256,1,128]{2,0,1:T(8,128)(2,1)S(1)}, u32[]{:S(2)}, u32[]{:S(2)}) collective-permute-start(bf16[256,1,128]{2,0,1:T(8,128)(2,1)S(1)} %fusion.115), channel_id=1, source_target_pairs={{0,4},{4,8},{8,12},{12,16},{16,20},{20,24},{24,28},{28,0},{1,5},{5... | collective-permute-start | bytes 196616 | tf_op jit(solution)/shard_map/while/body/eval_jaxpr/ppermute | solution.py:14
  133.7 5.7 %collective-permute-start.5 = (bf16[256,1,128]{2,0,1:T(8,128)(2,1)S(1)}, bf16[256,1,128]{2,0,1:T(8,128)(2,1)S(1)}, u32[]{:S(2)}, u32[]{:S(2)}) collective-permute-start(bf16[256,1,128]{2,0,1:T(8,128)(2,1)S(1)} %fusion.116), channel_id=1, source_target_pairs={{0,4},{4,8},{8,12},{12,16},{16,20},{20,24},{24,28},{28,0},{1,5},{5... | collective-permute-start | bytes 196616 | tf_op jit(solution)/shard_map/while/body/eval_jaxpr/ppermute | solution.py:14
  139.5 11.1 %collective-permute-start.2 = (bf16[256,1,128]{2,0,1:T(8,128)(2,1)S(1)}, bf16[256,1,128]{2,0,1:T(8,128)(2,1)S(1)}, u32[]{:S(2)}, u32[]{:S(2)}) collective-permute-start(bf16[256,1,128]{2,0,1:T(8,128)(2,1)S(1)} %copy.167), channel_id=1, source_target_pairs={{0,4},{4,8},{8,12},{12,16},{16,20},{20,24},{24,28},{28,0},{1,5},{5... | collective-permute-start | bytes 196616 | tf_op jit(solution)/shard_map/while/body/eval_jaxpr/ppermute | solution.py:14
  139.6 11.0 %collective-permute-start.3 = (bf16[256,1,128]{2,0,1:T(8,128)(2,1)S(1)}, bf16[256,1,128]{2,0,1:T(8,128)(2,1)S(1)}, u32[]{:S(2)}, u32[]{:S(2)}) collective-permute-start(bf16[256,1,128]{2,0,1:T(8,128)(2,1)S(1)} %copy.168), channel_id=1, source_target_pairs={{0,4},{4,8},{8,12},{12,16},{16,20},{20,24},{24,28},{28,0},{1,5},{5... | collective-permute-start | bytes 196616 | tf_op jit(solution)/shard_map/while/body/eval_jaxpr/ppermute | solution.py:14
  144.3 5.5 %collective-permute-start.4 = (bf16[256,1,128]{2,0,1:T(8,128)(2,1)S(1)}, bf16[256,1,128]{2,0,1:T(8,128)(2,1)S(1)}, u32[]{:S(2)}, u32[]{:S(2)}) collective-permute-start(bf16[256,1,128]{2,0,1:T(8,128)(2,1)S(1)} %fusion.115), channel_id=1, source_target_pairs={{0,4},{4,8},{8,12},{12,16},{16,20},{20,24},{24,28},{28,0},{1,5},{5... | collective-permute-start | bytes 196616 | tf_op jit(solution)/shard_map/while/body/eval_jaxpr/ppermute | solution.py:14
  144.8 5.7 %collective-permute-start.5 = (bf16[256,1,128]{2,0,1:T(8,128)(2,1)S(1)}, bf16[256,1,128]{2,0,1:T(8,128)(2,1)S(1)}, u32[]{:S(2)}, u32[]{:S(2)}) collective-permute-start(bf16[256,1,128]{2,0,1:T(8,128)(2,1)S(1)} %fusion.116), channel_id=1, source_target_pairs={{0,4},{4,8},{8,12},{12,16},{16,20},{20,24},{24,28},{28,0},{1,5},{5... | collective-permute-start | bytes 196616 | tf_op jit(solution)/shard_map/while/body/eval_jaxpr/ppermute | solution.py:14
  150.6 11.1 %collective-permute-start.2 = (bf16[256,1,128]{2,0,1:T(8,128)(2,1)S(1)}, bf16[256,1,128]{2,0,1:T(8,128)(2,1)S(1)}, u32[]{:S(2)}, u32[]{:S(2)}) collective-permute-start(bf16[256,1,128]{2,0,1:T(8,128)(2,1)S(1)} %copy.167), channel_id=1, source_target_pairs={{0,4},{4,8},{8,12},{12,16},{16,20},{20,24},{24,28},{28,0},{1,5},{5... | collective-permute-start | bytes 196616 | tf_op jit(solution)/shard_map/while/body/eval_jaxpr/ppermute | solution.py:14
  150.7 11.0 %collective-permute-start.3 = (bf16[256,1,128]{2,0,1:T(8,128)(2,1)S(1)}, bf16[256,1,128]{2,0,1:T(8,128)(2,1)S(1)}, u32[]{:S(2)}, u32[]{:S(2)}) collective-permute-start(bf16[256,1,128]{2,0,1:T(8,128)(2,1)S(1)} %copy.168), channel_id=1, source_target_pairs={{0,4},{4,8},{8,12},{12,16},{16,20},{20,24},{24,28},{28,0},{1,5},{5... | collective-permute-start | bytes 196616 | tf_op jit(solution)/shard_map/while/body/eval_jaxpr/ppermute | solution.py:14
  156.0 5.7 %collective-permute-start.5 = (bf16[256,1,128]{2,0,1:T(8,128)(2,1)S(1)}, bf16[256,1,128]{2,0,1:T(8,128)(2,1)S(1)}, u32[]{:S(2)}, u32[]{:S(2)}) collective-permute-start(bf16[256,1,128]{2,0,1:T(8,128)(2,1)S(1)} %fusion.116), channel_id=1, source_target_pairs={{0,4},{4,8},{8,12},{12,16},{16,20},{20,24},{24,28},{28,0},{1,5},{5... | collective-permute-start | bytes 196616 | tf_op jit(solution)/shard_map/while/body/eval_jaxpr/ppermute | solution.py:14
  161.8 11.1 %collective-permute-start.2 = (bf16[256,1,128]{2,0,1:T(8,128)(2,1)S(1)}, bf16[256,1,128]{2,0,1:T(8,128)(2,1)S(1)}, u32[]{:S(2)}, u32[]{:S(2)}) collective-permute-start(bf16[256,1,128]{2,0,1:T(8,128)(2,1)S(1)} %copy.167), channel_id=1, source_target_pairs={{0,4},{4,8},{8,12},{12,16},{16,20},{20,24},{24,28},{28,0},{1,5},{5... | collective-permute-start | bytes 196616 | tf_op jit(solution)/shard_map/while/body/eval_jaxpr/ppermute | solution.py:14
  161.9 11.0 %collective-permute-start.3 = (bf16[256,1,128]{2,0,1:T(8,128)(2,1)S(1)}, bf16[256,1,128]{2,0,1:T(8,128)(2,1)S(1)}, u32[]{:S(2)}, u32[]{:S(2)}) collective-permute-start(bf16[256,1,128]{2,0,1:T(8,128)(2,1)S(1)} %copy.168), channel_id=1, source_target_pairs={{0,4},{4,8},{8,12},{12,16},{16,20},{20,24},{24,28},{28,0},{1,5},{5... | collective-permute-start | bytes 196616 | tf_op jit(solution)/shard_map/while/body/eval_jaxpr/ppermute | solution.py:14
  166.6 5.5 %collective-permute-start.4 = (bf16[256,1,128]{2,0,1:T(8,128)(2,1)S(1)}, bf16[256,1,128]{2,0,1:T(8,128)(2,1)S(1)}, u32[]{:S(2)}, u32[]{:S(2)}) collective-permute-start(bf16[256,1,128]{2,0,1:T(8,128)(2,1)S(1)} %fusion.115), channel_id=1, source_target_pairs={{0,4},{4,8},{8,12},{12,16},{16,20},{20,24},{24,28},{28,0},{1,5},{5... | collective-permute-start | bytes 196616 | tf_op jit(solution)/shard_map/while/body/eval_jaxpr/ppermute | solution.py:14
  167.1 5.7 %collective-permute-start.5 = (bf16[256,1,128]{2,0,1:T(8,128)(2,1)S(1)}, bf16[256,1,128]{2,0,1:T(8,128)(2,1)S(1)}, u32[]{:S(2)}, u32[]{:S(2)}) collective-permute-start(bf16[256,1,128]{2,0,1:T(8,128)(2,1)S(1)} %fusion.116), channel_id=1, source_target_pairs={{0,4},{4,8},{8,12},{12,16},{16,20},{20,24},{24,28},{28,0},{1,5},{5... | collective-permute-start | bytes 196616 | tf_op jit(solution)/shard_map/while/body/eval_jaxpr/ppermute | solution.py:14
  172.9 11.1 %collective-permute-start.2 = (bf16[256,1,128]{2,0,1:T(8,128)(2,1)S(1)}, bf16[256,1,128]{2,0,1:T(8,128)(2,1)S(1)}, u32[]{:S(2)}, u32[]{:S(2)}) collective-permute-start(bf16[256,1,128]{2,0,1:T(8,128)(2,1)S(1)} %copy.167), channel_id=1, source_target_pairs={{0,4},{4,8},{8,12},{12,16},{16,20},{20,24},{24,28},{28,0},{1,5},{5... | collective-permute-start | bytes 196616 | tf_op jit(solution)/shard_map/while/body/eval_jaxpr/ppermute | solution.py:14
  173.0 11.0 %collective-permute-start.3 = (bf16[256,1,128]{2,0,1:T(8,128)(2,1)S(1)}, bf16[256,1,128]{2,0,1:T(8,128)(2,1)S(1)}, u32[]{:S(2)}, u32[]{:S(2)}) collective-permute-start(bf16[256,1,128]{2,0,1:T(8,128)(2,1)S(1)} %copy.168), channel_id=1, source_target_pairs={{0,4},{4,8},{8,12},{12,16},{16,20},{20,24},{24,28},{28,0},{1,5},{5... | collective-permute-start | bytes 196616 | tf_op jit(solution)/shard_map/while/body/eval_jaxpr/ppermute | solution.py:14
  177.7 5.5 %collective-permute-start.4 = (bf16[256,1,128]{2,0,1:T(8,128)(2,1)S(1)}, bf16[256,1,128]{2,0,1:T(8,128)(2,1)S(1)}, u32[]{:S(2)}, u32[]{:S(2)}) collective-permute-start(bf16[256,1,128]{2,0,1:T(8,128)(2,1)S(1)} %fusion.115), channel_id=1, source_target_pairs={{0,4},{4,8},{8,12},{12,16},{16,20},{20,24},{24,28},{28,0},{1,5},{5... | collective-permute-start | bytes 196616 | tf_op jit(solution)/shard_map/while/body/eval_jaxpr/ppermute | solution.py:14
  178.3 5.7 %collective-permute-start.5 = (bf16[256,1,128]{2,0,1:T(8,128)(2,1)S(1)}, bf16[256,1,128]{2,0,1:T(8,128)(2,1)S(1)}, u32[]{:S(2)}, u32[]{:S(2)}) collective-permute-start(bf16[256,1,128]{2,0,1:T(8,128)(2,1)S(1)} %fusion.116), channel_id=1, source_target_pairs={{0,4},{4,8},{8,12},{12,16},{16,20},{20,24},{24,28},{28,0},{1,5},{5... | collective-permute-start | bytes 196616 | tf_op jit(solution)/shard_map/while/body/eval_jaxpr/ppermute | solution.py:14
  185.9 8.1 %all-to-all-start.2 = ((bf16[4,2,4096]{2,1,0:T(2,128)(2,1)}), bf16[4,2,4096]{2,1,0:T(2,128)(2,1)S(1)}, u32[]{:S(2)}, u32[]{:S(2)}) async-start(bf16[4,2,4096]{2,1,0:T(2,128)(2,1)} %reshape.650), calls=%async_computation.2 | async-start | bytes 131072 | tf_op jit(solution)/shard_map/all_to_all | solution.py:164
  194.0 8.1 %all-to-all-start.3 = ((bf16[4,2,4096]{2,1,0:T(2,128)(2,1)}), bf16[4,2,4096]{2,1,0:T(2,128)(2,1)S(1)}, u32[]{:S(2)}, u32[]{:S(2)}) async-start(bf16[4,2,4096]{2,1,0:T(2,128)(2,1)} %reshape.652), calls=%async_computation.3 | async-start | bytes 131072 | tf_op jit(solution)/shard_map/all_to_all | solution.py:165
  (12 other events, 95.1 us)
